TPU v7x, 32 devices: a whole 2x2x4 slice. The times are simulated.
32 devices in a mesh: section: 2 (over core), seq: 2 (over x), head: 8 (over z, y).
Axes of the slice: x: 2, y: 2, z: 4, core: 2. Of those that a mesh axis runs over, the one named last changes fastest.
Arguments:
- hidden: bfloat16 [2, 512, 4096], P('section', 'seq', 'head'), may hold values from -6 to 6
- gain: bfloat16 [2, 4096], P('section'), may hold values from 0.5 to 1.5
- w_query: bfloat16 [2, 4096, 2048], P('section', None, 'head'), may hold values from -0.0234375 to 0.0234375
- w_key: bfloat16 [2, 4096, 2048], P('section', None, 'head'), may hold values from -0.09375 to 0.09375
- w_value: bfloat16 [2, 4096, 2048], P('section', None, 'head'), may hold values from -0.09375 to 0.09375
- w_out: bfloat16 [2, 2048, 4096], P('section', 'head'), may hold values from -0.5 to 0.5
- memory: bfloat16 [384, 4096], P(('section', 'seq', 'head')), may hold values from -6 to 6
- keep: int32 [384], P(('section', 'seq', 'head')), may hold values 0 or 1
Outputs:
- next_inputs: bfloat16 [2, 512, 4096], P('section', 'seq', 'head')
All inputs are finite; a program needn't handle non-finite values. No bound on the sum of `keep` on one device may be relied on, other than what follows from the above.
Results may differ from a plain program's by a relative error of at most 0.014.
Values may be sent and summed in bfloat16 or wider, within the bound.
A program may use at most 64 MiB of HBM per device.

v0:
```python
import jax
import jax.numpy as jnp
from jax import lax
from jax.sharding import PartitionSpec as P

HEAD_DIM = 64


mask_drop = 30.0
norm_eps = 1e-06


def from_behind(x, axis, by):
    length = lax.axis_size(axis)
    return lax.ppermute(x, axis, [(i, (i + by) % length) for i in range(length)])


def attend_terms(query, key_rows, value_rows, key_flags):
    head_count = query.shape[1] // HEAD_DIM
    query_heads = query.reshape(query.shape[0], head_count, HEAD_DIM)
    key_heads = key_rows.reshape(key_rows.shape[0], head_count, HEAD_DIM)
    value_heads = value_rows.reshape(value_rows.shape[0], head_count, HEAD_DIM)
    scores = jnp.einsum("qhd,khd->hqk", query_heads, key_heads, preferred_element_type=jnp.float32)
    scores = scores + ((key_flags.astype(jnp.float32) - 1.0) * mask_drop)[None, None, :]
    weights = jnp.exp(scores)
    numerator = jnp.einsum(
        "hqk,khd->qhd",
        weights.astype(jnp.bfloat16),
        value_heads,
        preferred_element_type=jnp.float32,
    )
    denominator = jnp.sum(weights, axis=2).T
    return (numerator.reshape(query.shape[0], head_count * HEAD_DIM), denominator)


def shards(hidden, gain, w_query, w_key, w_value, w_out, memory, keep):
    features = lax.all_gather(hidden[0], "head", axis=1, tiled=True)
    widened = features.astype(jnp.float32)
    inverse = lax.rsqrt(jnp.mean(widened * widened, axis=1, keepdims=True) + norm_eps)
    normed = (widened * inverse * gain[0].astype(jnp.float32)[None, :]).astype(jnp.bfloat16)
    query = jnp.dot(normed, w_query[0], preferred_element_type=jnp.float32).astype(jnp.bfloat16)
    encoder_rows, encoder_flags = (
        lax.all_gather(memory, ("section", "head"), axis=0, tiled=True),
        lax.all_gather(keep.astype(jnp.bfloat16), ("section", "head"), axis=0, tiled=True),
    )
    key_rows = jnp.dot(encoder_rows, w_key[0], preferred_element_type=jnp.float32).astype(
        jnp.bfloat16
    )
    value_rows = jnp.dot(encoder_rows, w_value[0], preferred_element_type=jnp.float32).astype(
        jnp.bfloat16
    )
    more_num, more_den = attend_terms(
        query,
        lax.all_gather(key_rows, "seq", axis=0, tiled=True),
        lax.all_gather(value_rows, "seq", axis=0, tiled=True),
        lax.all_gather(encoder_flags, "seq", axis=0, tiled=True),
    )
    spread = jnp.repeat(more_den, HEAD_DIM, axis=1)
    attended = (more_num / spread).astype(jnp.bfloat16)
    partial_terms = jnp.dot(attended, w_out[0], preferred_element_type=jnp.float32)
    update = lax.psum_scatter(
        partial_terms.astype(jnp.bfloat16), "head", scatter_dimension=1, tiled=True
    )
    moved = from_behind(update, "section", 1)
    return moved[None]


def solution(mesh):
    in_specs = (
        P("section", "seq", "head"),
        P("section", None),
        P("section", None, "head"),
        P("section", None, "head"),
        P("section", None, "head"),
        P("section", "head", None),
        P(("section", "seq", "head"), None),
        P(("section", "seq", "head")),
    )
    out_specs = P("section", "seq", "head")
    return jax.shard_map(shards, mesh=mesh, in_specs=in_specs, out_specs=out_specs, check_vma=False)
```

profile of v0, /device:TPU:1, one launch (start us, length us, event | category | flops | bytes accessed | tf_op | source)
XLA Modules:
  0.0 189.2 jit_solution(1261512691383816122)
XLA Ops:
  6.5 0.7 all-gather.7.cloned.1.call-update
  7.3 0.7 all-gather.5.cloned.1.call-update
  8.1 0.7 mul.39
  8.8 0.7 convert_element_type.40
  9.5 1.2 dynamic-slice
  10.7 1.2 dynamic-slice.1
  13.5 35.5 %all-reduce = bf16[192]{0:T(256)(128)(2,1)S(1)} all-reduce(bf16[192]{0:T(256)(128)(2,1)S(1)} %dynamic-update-slice), channel_id=1, replica_groups=mesh['section'=2,'seq'=2,'head'=8] {'section','head'}, use_global_device_ids=true, to_apply=%add | all-reduce | flops 192 | bytes 768
  49.2 3.8 %all-reduce.1 = bf16[384]{0:T(512)(128)(2,1)S(1)} all-reduce(bf16[384]{0:T(512)(128)(2,1)S(1)} %dynamic-update-slice.1), channel_id=1, replica_groups=mesh['section'=2,'seq'=2,'head'=8] {'seq'}, use_global_device_ids=true, to_apply=%add.1 | all-reduce | flops 384 | bytes 1536
  52.9 0.6 all-gather.7.cloned.1.call-done
  53.6 3.6 %reshape.34 = bf16[192,4096]{1,0:T(8,128)(2,1)} reshape(bf16[16,12,4096]{2,1,0:T(8,128)(2,1)} %all-gather.7.cloned.1.call-done) | data formatting | bytes 3145728
  57.1 2.6 %fusion.24 = bf16[192,256]{1,0:T(8,128)(2,1)S(1)} fusion(bf16[192,4096]{1,0:T(8,128)(2,1)} %reshape.34, bf16[1,4096,256]{2,1,0:T(8,128)(2,1)} %param.11), kind=kOutput, calls=%fused_computation.22 | convolution fusion | flops 402702336 | bytes 3768320 | tf_op jit(solution)/shard_map/dot_general | solution.py:46
  59.8 4.1 %all_gather.21 = bf16[384,256]{1,0:T(8,128)(2,1)S(1)} all-gather(bf16[192,256]{1,0:T(8,128)(2,1)S(1)} %fusion.24), channel_id=1, replica_groups=mesh['section'=2,'seq'=2,'head'=8] {'seq'}, dimensions={0}, use_global_device_ids=true | all-gather | bytes 294912 | tf_op jit(solution)/shard_map/all_gather | solution.py:54
  64.1 2.6 %fusion.21 = bf16[192,256]{1,0:T(8,128)(2,1)S(1)} fusion(bf16[192,4096]{1,0:T(8,128)(2,1)} %reshape.34, bf16[1,4096,256]{2,1,0:T(8,128)(2,1)} %param.12), kind=kOutput, calls=%fused_computation.21 | convolution fusion | flops 402702336 | bytes 3768320 | tf_op jit(solution)/shard_map/dot_general | solution.py:49
  66.8 4.1 %all_gather.19 = bf16[384,256]{1,0:T(8,128)(2,1)S(1)} all-gather(bf16[192,256]{1,0:T(8,128)(2,1)S(1)} %fusion.21), channel_id=1, replica_groups=mesh['section'=2,'seq'=2,'head'=8] {'seq'}, dimensions={0}, use_global_device_ids=true | all-gather | bytes 294912 | tf_op jit(solution)/shard_map/all_gather | solution.py:55
  71.1 33.5 %all-gather.5.cloned.1.call-done = bf16[1,256,4096]{2,1,0:T(8,128)(2,1)} async-done(((bf16[1,256,512]{2,1,0:T(8,128)(2,1)}), bf16[1,256,4096]{2,1,0:T(8,128)(2,1)}) %all-gather.5.cloned.1.call-update) | async-done | bytes 2097168 | tf_op jit(solution)/shard_map/all_gather | solution.py:37
  104.6 2.2 %fusion = f32[256]{0:T(256)S(1)} fusion(bf16[1,256,4096]{2,1,0:T(8,128)(2,1)} %all-gather.5.cloned.1.call-done), kind=kLoop, calls=%fused_computation.3 | loop fusion | flops 3145472 | bytes 2098176 | tf_op jit(solution)/shard_map/reduce_sum | solution.py:39
  106.8 2.8 %fusion.16 = bf16[256,256]{0,1:T(8,128)(2,1)S(1)} fusion(bf16[1,4096,256]{2,1,0:T(8,128)(2,1)} %param.10, bf16[1,256,4096]{2,1,0:T(8,128)(2,1)S(1)} %copy-done.1, f32[4096]{0:T(1024)S(1)} %bitcast.55, f32[256]{0:T(256)S(1)} %add_rsqrt_fusion), kind=kOutput, calls=%fused_computation.20 | convolution fusion | flops 541130752 | bytes 4342784 | tf_op jit(solution)/shard_map/dot_general | solution.py:41
  109.6 0.5 fusion.28
  110.2 0.4 fusion.15
  110.5 2.1 %convolution_convert_fusion = bf16[256,4096]{1,0:T(8,128)(2,1)} fusion(bf16[256,256]{0,1:T(8,128)(2,1)S(1)} %bitcast.53, bf16[1,256,4096]{2,1,0:T(8,128)(2,1)S(1)} %copy-done), kind=kOutput, calls=%fused_computation.2 | convolution fusion | flops 537919488 | bytes 4325376 | tf_op jit(solution)/shard_map/dot_general | solution.py:60
  112.7 65.5 %reduce-scatter.2.cloned.1.call-done = bf16[256,512]{1,0:T(8,128)(2,1)} async-done(((bf16[256,4096]{1,0:T(8,128)(2,1)}), bf16[256,512]{1,0:T(8,128)(2,1)}) %reduce-scatter.2.cloned.1.call-update) | async-done | bytes 262160 | tf_op jit(solution)/shard_map/reduce_scatter | solution.py:61
  178.1 2.4 %collective-permute-start = (bf16[256,512]{1,0:T(8,128)(2,1)}, bf16[256,512]{1,0:T(8,128)(2,1)S(1)}, u32[]{:S(2)}, u32[]{:S(2)}) collective-permute-start(bf16[256,512]{1,0:T(8,128)(2,1)} %reduce-scatter.2.cloned.1.call-done), channel_id=1, source_target_pairs={{0,16},{16,0},{1,17},{17,1},{2,18},{18,2},{3,19},{19,3},{4,20},{20... | collective-permute-start | bytes 786440 | tf_op jit(solution)/shard_map/ppermute | solution.py:15
  180.6 1.4 collective-permute-done
  181.9 0.7 copy.18
  (16 shorter events, 0.9 us)
Async XLA Ops:
  6.5 104.0 %copy-start = (bf16[1,256,4096]{2,1,0:T(8,128)(2,1)S(1)}, bf16[1,256,4096]{2,1,0:T(8,128)(2,1)}, u32[]{:S(2)}) copy-start(bf16[1,256,4096]{2,1,0:T(8,128)(2,1)} %param.13) | copy-start | bytes 6291460
  6.5 47.0 %all-gather.7.cloned.1.call-start = ((), (), s32[]{:S(2)}) async-start(), calls=%async_computation.3 | async-start | bytes 2228224 | tf_op jit(solution)/shard_map/all_gather | solution.py:43
  7.3 97.3 %all-gather.5.cloned.1.call-start = ((), (), s32[]{:S(2)}) async-start(), calls=%async_computation.2 | async-start | bytes 2359296 | tf_op jit(solution)/shard_map/all_gather | solution.py:37
  8.0 170.1 %reduce-scatter.2.cloned.1.call-start = ((), (), s32[]{:S(2)}) async-start(), calls=%async_computation.1 | async-start | bytes 2359296 | tf_op jit(solution)/shard_map/reduce_scatter | solution.py:61
  104.6 2.2 %copy-start.1 = (bf16[1,256,4096]{2,1,0:T(8,128)(2,1)S(1)}, bf16[1,256,4096]{2,1,0:T(8,128)(2,1)}, u32[]{:S(2)}) copy-start(bf16[1,256,4096]{2,1,0:T(8,128)(2,1)} %all-gather.5.cloned.1.call-done) | copy-start | bytes 6291460
  178.1 3.8 %collective-permute-start = (bf16[256,512]{1,0:T(8,128)(2,1)}, bf16[256,512]{1,0:T(8,128)(2,1)S(1)}, u32[]{:S(2)}, u32[]{:S(2)}) collective-permute-start(bf16[256,512]{1,0:T(8,128)(2,1)} %reduce-scatter.2.cloned.1.call-done), channel_id=1, source_target_pairs={{0,16},{16,0},{1,17},{17,1},{2,18},{18,2},{3,19},{19,3},{4,20},{20... | collective-permute-start | bytes 786440 | tf_op jit(solution)/shard_map/ppermute | solution.py:15
Sparse Core Ops, SparseCore 0:
  9.6 43.9 all-gather.6
  55.6 48.9 all-gather.4
  112.8 65.3 reduce-scatter.1
where the time goes:
time: 190 us; the launch traced here: 189 us
  waiting for transfers between devices  102 us (54%)
  blocking collectives  47.5 us (25%)
  between operations  14.4 us (8%)
  matrix products  11.1 us (6%)
  local copies, waits for them, and re-layouts  7.59 us (4%)
  other arithmetic  3.65 us (2%)
  starting transfers between devices  2.5 us (1%)
    reduce_scatter x1, waiting for transfers between devices, shards(): lax.psum_scatter(partial_terms.astype(jnp.bfloat16), 'head', scatter_dime...  65.5 us
    unnamed x2, blocking collectives  39.2 us
    all_gather x1, waiting for transfers between devices, shards(): features = lax.all_gather(hidden[0], 'head', axis=1, tiled=True)  33.5 us
    unnamed x12, local copies, waits for them, and re-layouts  7.26 us
    all_gather x1, blocking collectives, shards(): lax.all_gather(value_rows, 'seq', axis=0, tiled=True)  4.14 us
    all_gather x1, blocking collectives, shards(): lax.all_gather(key_rows, 'seq', axis=0, tiled=True)  4.14 us
  transfers between devices with their start and end apart: 4, of which 4 were waited for; matrix products, arithmetic and copies ran while one was open for 7% of the time, Pallas kernels for 0%

commit v1 on v0

v1 whole, which is shorter than its diff:
```python
import functools

import jax
import jax.numpy as jnp
from jax import lax
from jax.experimental import pallas as pl
from jax.experimental.pallas import tpu as pltpu
from jax.sharding import PartitionSpec as P

HEAD_DIM = 64
SIDES = 2
CHUNKS = 2

mask_drop = 30.0
norm_eps = 1e-06

MESH = pl.DeviceIdType.MESH


def wrap(value, length):
    return lax.rem(value, length)


def kernel(
    sections,
    seqs,
    heads,
    rows_each,
    hidden_ref,
    gain_ref,
    wq_ref,
    wk_ref,
    wv_ref,
    wo_ref,
    mem_ref,
    out_ref,
    hid,
    gain,
    wq,
    wk,
    wv,
    wo,
    mem,
    raw,
    kv,
    att,
    side_send,
    side_recv,
    line_send,
    line_recv,
    load_sem,
    hid_send,
    hid_recv,
    mem_send,
    mem_recv,
    kv_send,
    kv_recv,
    side_ssem,
    side_rsem,
    line_ssem,
    line_rsem,
):
    s, q, h = lax.axis_index("section"), lax.axis_index("seq"), lax.axis_index("head")
    lines = heads // SIDES
    line, side = h // SIDES, lax.rem(h, SIDES)
    other = 1 - side
    partner = line * SIDES + other
    tokens = hid.shape[2]
    width = hid.shape[3]
    inner = wq.shape[1]
    padded = mem.shape[2]
    next_s, prev_s = wrap(s + 1, sections), wrap(s + sections - 1, sections)

    def near(k):
        return wrap(line + k, lines)

    def at(ls):
        return ls * SIDES + side

    def opposite(ls):
        return ls * SIDES + other

    loads = {}

    def load(name, index, src, dst):
        loads[name] = pltpu.make_async_copy(src, dst, load_sem.at[index])
        loads[name].start()

    load("mem", 0, mem_ref, mem.at[s, h])
    for c in range(CHUNKS):
        load(("hid", c), 1 + c, hidden_ref.at[pl.ds(c * tokens, tokens)], hid.at[c, h])
    load("wk", 1 + CHUNKS, wk_ref, wk)
    load("wv", 2 + CHUNKS, wv_ref, wv)
    load("wq", 3 + CHUNKS, wq_ref, wq)
    load("gain", 4 + CHUNKS, gain_ref, gain)
    load("wo", 5 + CHUNKS, wo_ref, wo)

    barrier = pltpu.get_barrier_semaphore()
    peers = [(s, q, at(near(k))) for k in range(1, lines)] + [(s, q, partner)]
    peers += [(wrap(s + k, sections), q, h) for k in range(1, sections)]
    peers += [(s, wrap(q + k, seqs), h) for k in range(1, seqs)]
    peers += [(next_s, q, at(near(k))) for k in range(1, lines)]
    if sections > 2:
        peers += [(prev_s, q, at(near(k))) for k in range(1, lines)]
    for peer in peers:
        pl.semaphore_signal(barrier, inc=1, device_id=peer, device_id_type=MESH)
    pl.semaphore_wait(barrier, len(peers))

    sent = []

    def send(src, dst, ssem, rsem, device):
        copy = pltpu.make_async_remote_copy(
            src_ref=src, dst_ref=dst, send_sem=ssem, recv_sem=rsem,
            device_id=device, device_id_type=MESH,
        )
        copy.start()
        sent.append(copy)

    def arrived(dst, ssem, rsem):
        pltpu.make_async_remote_copy(
            src_ref=dst, dst_ref=dst, send_sem=ssem, recv_sem=rsem,
            device_id=(s, q, partner), device_id_type=MESH,
        ).wait_recv()

    def mem_out(block, slot, device, index):
        send(block, mem.at[s, slot], mem_send.at[index], mem_recv.at[s, slot], device)

    def mem_across(block, slot, j):
        base = lines - 1 + lines
        for k in range(1, sections):
            mem_out(block, slot, (wrap(s + k, sections), q, h), base + j * (sections - 1) + k - 1)

    def hid_lines(c):
        rows = hidden_ref.at[pl.ds(c * tokens, tokens)]
        for k in range(1, lines):
            send(rows, hid.at[c, h], hid_send.at[c, k - 1], hid_recv.at[c, h], (s, q, at(near(k))))
        send(rows, hid.at[c, h], hid_send.at[c, lines - 1], hid_recv.at[c, h], (s, q, partner))

    def hid_forward(c):
        for k in range(1, lines):
            slot = at(near(lines - k))
            arrived(hid.at[c, slot], hid_send.at[c, 0], hid_recv.at[c, slot])
            send(hid.at[c, slot], hid.at[c, slot], hid_send.at[c, lines - 1 + k],
                 hid_recv.at[c, slot], (s, q, partner))

    for k in range(1, lines):
        mem_out(mem_ref, h, (s, q, at(near(k))), k - 1)
    mem_out(mem_ref, h, (s, q, partner), lines - 1)
    mem_across(mem_ref, h, 0)
    hid_lines(0)
    for k in range(1, lines):
        slot = at(near(lines - k))
        arrived(mem.at[s, slot], mem_send.at[0], mem_recv.at[s, slot])
        mem_out(mem.at[s, slot], slot, (s, q, partner), lines - 1 + k)
        mem_across(mem.at[s, slot], slot, k)
    hid_forward(0)
    for c in range(1, CHUNKS):
        hid_lines(c)
    for k in range(lines):
        slot = opposite(near(lines - k))
        arrived(mem.at[s, slot], mem_send.at[0], mem_recv.at[s, slot])
        mem_across(mem.at[s, slot], slot, lines + k)

    loads["mem"].wait()
    loads["wk"].wait()
    loads["wv"].wait()
    block_rows = heads * padded

    def project(sj):
        rows = mem[sj].reshape(block_rows, mem.shape[3])
        into = pl.ds(pl.multiple_of(sj * block_rows, block_rows), block_rows)
        raw[into, :inner] = jnp.dot(rows, wk[...], preferred_element_type=jnp.float32).astype(jnp.bfloat16)
        raw[into, inner : 2 * inner] = jnp.dot(
            rows, wv[...], preferred_element_type=jnp.float32
        ).astype(jnp.bfloat16)
        raw[into, 2 * inner :] = rows[:, :128]

    project(s)
    for k in range(1, sections):
        sj = wrap(s + k, sections)
        for hj in range(heads):
            arrived(mem.at[sj, hj], mem_send.at[0], mem_recv.at[sj, hj])
        project(sj)
    shard = sections * heads * rows_each
    total_raw = sections * block_rows
    row = lax.broadcasted_iota(jnp.int32, (shard, total_raw), 0)
    col = lax.broadcasted_iota(jnp.int32, (shard, total_raw), 1)
    owner, place = row // rows_each, row % rows_each
    pick = (col == owner * padded + place).astype(jnp.bfloat16)
    pick_flags = (col == owner * padded + rows_each).astype(jnp.bfloat16)
    mine = pl.ds(pl.multiple_of(q * shard, shard), shard)
    kv[mine, : 2 * inner] = jnp.dot(
        pick, raw[:, : 2 * inner], preferred_element_type=jnp.float32
    ).astype(jnp.bfloat16)
    flags = jnp.dot(pick_flags, raw[:, 2 * inner :], preferred_element_type=jnp.float32)
    lane = lax.broadcasted_iota(jnp.int32, (shard, 128), 1)
    own_place = lax.broadcasted_iota(jnp.int32, (shard, 128), 0) % rows_each
    kv[mine, 2 * inner :] = jnp.where(lane == own_place, flags, 0.0).astype(jnp.bfloat16)
    for k in range(1, seqs):
        send(kv.at[mine], kv.at[mine], kv_send.at[k - 1], kv_recv.at[q], (s, wrap(q + k, seqs), h))

    head_of = lax.broadcasted_iota(jnp.int32, (tokens, inner), 1) // HEAD_DIM

    def query_of(c):
        total = jnp.zeros((tokens, inner), jnp.float32)
        squares = jnp.zeros((tokens, 1), jnp.float32)
        order = [h] + [at(near(lines - k)) for k in range(1, lines)]
        order += [opposite(near(lines - k)) for k in range(lines)]
        for j, slot in enumerate(order):
            if j == 0:
                loads[("hid", c)].wait()
            elif j >= lines:
                arrived(hid.at[c, slot], hid_send.at[c, 0], hid_recv.at[c, slot])
            span = pl.ds(pl.multiple_of(slot * width, width), width)
            x = hid[c, slot].astype(jnp.float32)
            squares += jnp.sum(x * x, axis=1, keepdims=True)
            scaled = (x * gain[:, span].astype(jnp.float32)).astype(jnp.bfloat16)
            total += jnp.dot(scaled, wq[span, :], preferred_element_type=jnp.float32)
        inverse = lax.rsqrt(squares / (heads * width) + norm_eps)
        return (total * inverse).astype(jnp.bfloat16)

    def attend(c, query):
        ones = jnp.ones((8, 128), jnp.bfloat16)
        kept = lax.dot_general(
            ones, kv[:, 2 * inner :], (((1,), (1,)), ((), ())), preferred_element_type=jnp.float32
        )
        bias = (kept[:1] - 1.0) * mask_drop
        attended = jnp.zeros((tokens, inner), jnp.float32)
        for head in range(inner // HEAD_DIM):
            only = jnp.where(head_of == head, query, jnp.zeros_like(query))
            scores = lax.dot_general(
                only, kv[:, :inner], (((1,), (1,)), ((), ())), preferred_element_type=jnp.float32
            )
            weights = jnp.exp(scores + bias)
            denominator = jnp.sum(weights, axis=1, keepdims=True)
            numerator = jnp.dot(
                weights.astype(jnp.bfloat16), kv[:, inner : 2 * inner], preferred_element_type=jnp.float32
            )
            attended = jnp.where(head_of == head, numerator / denominator, attended)
        att[c] = attended.astype(jnp.bfloat16)

    def term(c, slot):
        span = pl.ds(pl.multiple_of(slot * width, width), width)
        return jnp.dot(att[c], wo[:, span], preferred_element_type=jnp.float32)

    def to_side(c):
        for k in range(lines):
            to = near(1 + k)
            side_send[c, k] = term(c, opposite(to)).astype(jnp.bfloat16)
            send(side_send.at[c, k], side_recv.at[c, to], side_ssem.at[c, k], side_rsem.at[c, to],
                 (s, q, partner))

    def to_lines(c):
        for k in range(lines):
            to = near(1 + k)
            own = term(c, at(to))
            arrived(side_recv.at[c, to], side_ssem.at[c, 0], side_rsem.at[c, to])
            line_send[c, k] = (own + side_recv[c, to].astype(jnp.float32)).astype(jnp.bfloat16)
            send(line_send.at[c, k], line_recv.at[c, line], line_ssem.at[c, k],
                 line_rsem.at[c, line], (next_s, q, at(to)))

    for c in range(CHUNKS):
        if c == 0:
            loads["wq"].wait()
            loads["gain"].wait()
        if c + 1 < CHUNKS:
            hid_forward(c + 1)
        query = query_of(c)
        if c == 0:
            for k in range(1, seqs):
                qj = wrap(q + k, seqs)
                theirs = kv.at[pl.ds(pl.multiple_of(qj * shard, shard), shard)]
                arrived(theirs, kv_send.at[0], kv_recv.at[qj])
        attend(c, query)
        if c == 0:
            loads["wo"].wait()
        to_side(c)
        if c >= 1:
            to_lines(c - 1)
    to_lines(CHUNKS - 1)
    for c in range(CHUNKS):
        update = jnp.zeros((tokens, width), jnp.float32)
        for ls in range(lines):
            arrived(line_recv.at[c, ls], line_ssem.at[c, 0], line_rsem.at[c, ls])
            update += line_recv[c, ls].astype(jnp.float32)
        out_ref[c * tokens : (c + 1) * tokens, :] = update.astype(jnp.bfloat16)
    for copy in sent:
        copy.wait_send()


def shards(sizes, hidden, gain, w_query, w_key, w_value, w_out, memory, keep):
    sections, seqs, heads = sizes
    lines = heads // SIDES
    all_tokens, width = hidden.shape[1:]
    tokens = all_tokens // CHUNKS
    rows_each, model = memory.shape
    padded = (rows_each + 1 + 15) // 16 * 16
    inner = w_query.shape[2]
    flags = jnp.pad(keep.astype(jnp.bfloat16)[None, :], ((0, 0), (0, model - rows_each)))
    block = jnp.concatenate(
        [memory, flags, jnp.zeros((padded - rows_each - 1, model), jnp.bfloat16)], axis=0
    )
    shard = sections * heads * rows_each
    low = jnp.bfloat16
    hbm = pl.BlockSpec(memory_space=pl.ANY)
    dma = pltpu.SemaphoreType.DMA
    return pl.pallas_call(
        functools.partial(kernel, sections, seqs, heads, rows_each),
        out_shape=jax.ShapeDtypeStruct((all_tokens, width), low),
        in_specs=[hbm] * 7,
        out_specs=pl.BlockSpec(memory_space=pltpu.VMEM),
        scratch_shapes=[
            pltpu.VMEM((CHUNKS, heads, tokens, width), low),
            pltpu.VMEM((1, model), low),
            pltpu.VMEM((model, inner), low),
            pltpu.VMEM((model, inner), low),
            pltpu.VMEM((model, inner), low),
            pltpu.VMEM((inner, model), low),
            pltpu.VMEM((sections, heads, padded, model), low),
            pltpu.VMEM((sections * heads * padded, 2 * inner + 128), low),
            pltpu.VMEM((seqs * shard, 2 * inner + 128), low),
            pltpu.VMEM((CHUNKS, tokens, inner), low),
            pltpu.VMEM((CHUNKS, lines, tokens, width), low),
            pltpu.VMEM((CHUNKS, lines, tokens, width), low),
            pltpu.VMEM((CHUNKS, lines, tokens, width), low),
            pltpu.VMEM((CHUNKS, lines, tokens, width), low),
            dma((6 + CHUNKS,)),
            dma((CHUNKS, 2 * lines - 1)),
            dma((CHUNKS, heads)),
            dma((2 * lines - 1 + heads * (sections - 1),)),
            dma((sections, heads)),
            dma((seqs,)),
            dma((seqs,)),
            dma((CHUNKS, lines)),
            dma((CHUNKS, lines)),
            dma((CHUNKS, lines)),
            dma((CHUNKS, lines)),
        ],
        compiler_params=pltpu.CompilerParams(
            collective_id=0, has_side_effects=True, vmem_limit_bytes=48 * 1024 * 1024
        ),
    )(hidden[0], gain, w_query[0], w_key[0], w_value[0], w_out[0], block)[None]


def solution(mesh):
    in_specs = (
        P("section", "seq", "head"),
        P("section", None),
        P("section", None, "head"),
        P("section", None, "head"),
        P("section", None, "head"),
        P("section", "head", None),
        P(("section", "seq", "head"), None),
        P(("section", "seq", "head")),
    )
    out_specs = P("section", "seq", "head")
    sizes = tuple(mesh.shape[name] for name in ("section", "seq", "head"))
    return jax.shard_map(
        functools.partial(shards, sizes),
        mesh=mesh, in_specs=in_specs, out_specs=out_specs, check_vma=False,
    )
```

time: 190 us -> 84.2 us (0.44)
  waiting for transfers between devices: 102 us -> 0 us
  Pallas kernels: 0 us -> 76 us
  blocking collectives: 47.5 us -> 0 us
  between operations: 14.4 us -> 0.02 us
  matrix products: 11.1 us -> 0 us
  starting transfers between devices: 2.5 us -> 0 us
  other arithmetic: 3.65 us -> 1.65 us
  local copies, waits for them, and re-layouts: 7.59 us -> 5.63 us
    pallas_call x0 -> x1, Pallas kernels: none -> 76 us  [shards(): pl.pallas_call(functools.partial(kernel, sections, seqs, heads, rows_each...]
    reduce_scatter x1 -> x0, waiting for transfers between devices: 65.5 us -> none  [shards(): lax.psum_scatter(partial_terms.astype(jnp.bfloat16), 'head', scatter_dime...]
    unnamed x2 -> x0, blocking collectives: 39.2 us -> none
    all_gather x2 -> x0, waiting for transfers between devices: 34.1 us -> none  [the longest x1 33.5 us: shards(): features = lax.all_gather(hidden[0], 'head', axis=1, tiled=True)]
    dot_general x6 -> x0, matrix products: 11.1 us -> none  [the longest x1 2.79 us: shards(): jnp.dot(normed, w_query[0], preferred_element_type=jnp.float32)]
    all_gather x2 -> x0, blocking collectives: 8.29 us -> none  [the longest x1 4.14 us: shards(): lax.all_gather(value_rows, 'seq', axis=0, tiled=True)]
    ppermute x1 -> x0, starting transfers between devices: 2.43 us -> none  [from_behind(): lax.ppermute(x, axis, [(i, (i + by) % length) for i in range(length)])]
    reduce_sum x1 -> x0, other arithmetic: 2.23 us -> none  [shards(): jnp.mean(widened * widened, axis=1, keepdims=True) + norm_eps]
  transfers between devices with their start and end apart: 4 -> 0, of which waited for: 4 -> 0; matrix products, arithmetic and copies ran while one was open for 7% -> 0% of each run, Pallas kernels for 0% -> 0%
where the time goes in v1:
time: 84.2 us; the launch traced here: 83.3 us
  Pallas kernels  76 us (90%)
  local copies, waits for them, and re-layouts  5.63 us (7%)
  other arithmetic  1.65 us (2%)
    pallas_call x1, Pallas kernels, shards(): pl.pallas_call(functools.partial(kernel, sections, seqs, heads, rows_each...  76 us
    unnamed x9, local copies, waits for them, and re-layouts  5.55 us

profile of v1, /device:TPU:1, one launch (start us, length us, event | category | flops | bytes accessed | tf_op | source)
XLA Modules:
  0.0 83.3 jit_solution(10035200025504720013)
XLA Ops:
  0.0 0.7 convert_bitcast_fusion
  0.7 0.1 pad.7.clone
  0.7 1.0 %fusion.3.mem_ref = bf16[16,4096]{1,0:T(8,128)(2,1)S(1)} fusion(bf16[1,12]{1,0:T(2,128)(2,1)S(1)} %convert_bitcast_fusion, bf16[12,4096]{1,0:T(8,128)(2,1)} %param.14, bf16[16]{0:T(256)(128)(2,1)S(1)} %pad.7.clone), kind=kLoop, calls=%fused_computation.5 | loop fusion | flops 655360 | bytes 229432 | tf_op jit(solution)/shard_map/concatenate | solution.py:300
  1.7 0.0 copy-start
  1.7 1.6 %copy-done = bf16[1,4096,256]{2,1,0:T(8,128)(2,1)S(1)} copy-done((bf16[1,4096,256]{2,1,0:T(8,128)(2,1)S(1)}, bf16[1,4096,256]{2,1,0:T(8,128)(2,1)}, u32[]{:S(2)}) %copy-start) | copy-done | bytes 2097176
  3.3 0.0 copy-start.1
  3.3 1.6 %copy-done.1 = bf16[1,4096,256]{2,1,0:T(8,128)(2,1)S(1)} copy-done((bf16[1,4096,256]{2,1,0:T(8,128)(2,1)S(1)}, bf16[1,4096,256]{2,1,0:T(8,128)(2,1)}, u32[]{:S(2)}) %copy-start.1) | copy-done | bytes 2097176
  4.9 0.0 copy-start.2
  4.9 0.9 %copy-done.2 = bf16[1,256,512]{2,1,0:T(8,128)(2,1)S(1)} copy-done((bf16[1,256,512]{2,1,0:T(8,128)(2,1)S(1)}, bf16[1,256,512]{2,1,0:T(8,128)(2,1)}, u32[]{:S(2)}) %copy-start.2) | copy-done | bytes 262168
  5.9 0.0 copy-start.3
  5.9 0.7 copy-done.3
  6.6 76.0 %shard_map.82 = bf16[256,512]{1,0:T(8,128)(2,1)S(1)} custom-call(bf16[256,512]{1,0:T(8,128)(2,1)S(1)} %bitcast.11, bf16[1,4096]{1,0:T(2,128)(2,1)S(1)} %copy-done.3, bf16[4096,256]{1,0:T(8,128)(2,1)S(1)} %bitcast.8, bf16[4096,256]{1,0:T(8,128)(2,1)S(1)} %bitcast.9, bf16[4096,256]{1,0:T(8,128)(2,1)} %bitcast.12, bf16[256,4096]{1,0:T(8,128)(2,1)} %bitcast.13, ...), custom_call_target="tpu_custom_call" | custom-call | tf_op jit(solution)/shard_map/pallas_call | solution.py:307
  82.6 0.7 copy.10
  (1 shorter events, 0.0 us)
Async XLA Ops:
  1.7 1.6 %copy-start = (bf16[1,4096,256]{2,1,0:T(8,128)(2,1)S(1)}, bf16[1,4096,256]{2,1,0:T(8,128)(2,1)}, u32[]{:S(2)}) copy-start(bf16[1,4096,256]{2,1,0:T(8,128)(2,1)} %param.10) | copy-start | bytes 6291460
  3.3 1.6 %copy-start.1 = (bf16[1,4096,256]{2,1,0:T(8,128)(2,1)S(1)}, bf16[1,4096,256]{2,1,0:T(8,128)(2,1)}, u32[]{:S(2)}) copy-start(bf16[1,4096,256]{2,1,0:T(8,128)(2,1)} %param.11) | copy-start | bytes 6291460
  4.9 0.9 %copy-start.2 = (bf16[1,256,512]{2,1,0:T(8,128)(2,1)S(1)}, bf16[1,256,512]{2,1,0:T(8,128)(2,1)}, u32[]{:S(2)}) copy-start(bf16[1,256,512]{2,1,0:T(8,128)(2,1)} %param.8) | copy-start | bytes 786436
  5.9 0.7 copy-start.3

commit v2 on v1

--- a/solution.py
+++ b/solution.py
@@ -9,7 +9,7 @@
 
 HEAD_DIM = 64
 SIDES = 2
-CHUNKS = 2
+CHUNKS = 4
 
 mask_drop = 30.0
 norm_eps = 1e-06
@@ -44,6 +44,8 @@
     raw,
     kv,
     att,
+    keys_t,
+    bias,
     side_send,
     side_recv,
     line_send,
@@ -89,12 +91,6 @@
     load("mem", 0, mem_ref, mem.at[s, h])
     for c in range(CHUNKS):
         load(("hid", c), 1 + c, hidden_ref.at[pl.ds(c * tokens, tokens)], hid.at[c, h])
-    load("wk", 1 + CHUNKS, wk_ref, wk)
-    load("wv", 2 + CHUNKS, wv_ref, wv)
-    load("wq", 3 + CHUNKS, wq_ref, wq)
-    load("gain", 4 + CHUNKS, gain_ref, gain)
-    load("wo", 5 + CHUNKS, wo_ref, wo)
-
     barrier = pltpu.get_barrier_semaphore()
     peers = [(s, q, at(near(k))) for k in range(1, lines)] + [(s, q, partner)]
     peers += [(wrap(s + k, sections), q, h) for k in range(1, sections)]
@@ -148,6 +144,11 @@
     mem_out(mem_ref, h, (s, q, partner), lines - 1)
     mem_across(mem_ref, h, 0)
     hid_lines(0)
+    load("wk", 1 + CHUNKS, wk_ref, wk)
+    load("wv", 2 + CHUNKS, wv_ref, wv)
+    load("wq", 3 + CHUNKS, wq_ref, wq)
+    load("gain", 4 + CHUNKS, gain_ref, gain)
+    load("wo", 5 + CHUNKS, wo_ref, wo)
     for k in range(1, lines):
         slot = at(near(lines - k))
         arrived(mem.at[s, slot], mem_send.at[0], mem_recv.at[s, slot])
@@ -185,21 +186,27 @@
     total_raw = sections * block_rows
     row = lax.broadcasted_iota(jnp.int32, (shard, total_raw), 0)
     col = lax.broadcasted_iota(jnp.int32, (shard, total_raw), 1)
-    owner, place = row // rows_each, row % rows_each
-    pick = (col == owner * padded + place).astype(jnp.bfloat16)
-    pick_flags = (col == owner * padded + rows_each).astype(jnp.bfloat16)
+    shift = padded.bit_length() - 1
+    owner, place = lax.shift_right_logical(col, shift), col & (padded - 1)
+    start = owner * rows_each
+    pick = ((row == start + place) & (place < rows_each)).astype(jnp.bfloat16)
+    pick_flags = ((row >= start) & (row < start + rows_each) & (place == rows_each)).astype(jnp.bfloat16)
     mine = pl.ds(pl.multiple_of(q * shard, shard), shard)
     kv[mine, : 2 * inner] = jnp.dot(
         pick, raw[:, : 2 * inner], preferred_element_type=jnp.float32
     ).astype(jnp.bfloat16)
     flags = jnp.dot(pick_flags, raw[:, 2 * inner :], preferred_element_type=jnp.float32)
     lane = lax.broadcasted_iota(jnp.int32, (shard, 128), 1)
-    own_place = lax.broadcasted_iota(jnp.int32, (shard, 128), 0) % rows_each
-    kv[mine, 2 * inner :] = jnp.where(lane == own_place, flags, 0.0).astype(jnp.bfloat16)
+    own_row = lax.broadcasted_iota(jnp.int32, (shard, 128), 0)
+    near_lane = jnp.zeros((shard, 128), jnp.bool_)
+    for j in range(sections * heads):
+        near_lane |= own_row == lane + j * rows_each
+    kv[mine, 2 * inner :] = jnp.where(near_lane & (lane < rows_each), flags, 0.0).astype(jnp.bfloat16)
     for k in range(1, seqs):
         send(kv.at[mine], kv.at[mine], kv_send.at[k - 1], kv_recv.at[q], (s, wrap(q + k, seqs), h))
 
     head_of = lax.broadcasted_iota(jnp.int32, (tokens, inner), 1) // HEAD_DIM
+    own_heads = inner // HEAD_DIM
 
     def query_of(c):
         total = jnp.zeros((tokens, inner), jnp.float32)
@@ -219,24 +226,27 @@
         inverse = lax.rsqrt(squares / (heads * width) + norm_eps)
         return (total * inverse).astype(jnp.bfloat16)
 
+    def prepare():
+        kept = lax.dot_general(
+            jnp.ones((8, 128), jnp.bfloat16), kv[:, 2 * inner :], (((1,), (1,)), ((), ())),
+            preferred_element_type=jnp.float32,
+        )
+        bias[...] = (kept - 1.0) * mask_drop
+        keys_t[...] = kv[:, :inner].T
+
     def attend(c, query):
-        ones = jnp.ones((8, 128), jnp.bfloat16)
-        kept = lax.dot_general(
-            ones, kv[:, 2 * inner :], (((1,), (1,)), ((), ())), preferred_element_type=jnp.float32
+        none = jnp.zeros_like(query)
+        stacked = jnp.concatenate([jnp.where(head_of == j, query, none) for j in range(own_heads)], axis=0)
+        scores = jnp.dot(stacked, keys_t[...], preferred_element_type=jnp.float32)
+        weights = jnp.exp(scores + bias[:1])
+        denominator = jnp.sum(weights, axis=1, keepdims=True)
+        numerator = jnp.dot(
+            weights.astype(jnp.bfloat16), kv[:, inner : 2 * inner], preferred_element_type=jnp.float32
         )
-        bias = (kept[:1] - 1.0) * mask_drop
-        attended = jnp.zeros((tokens, inner), jnp.float32)
-        for head in range(inner // HEAD_DIM):
-            only = jnp.where(head_of == head, query, jnp.zeros_like(query))
-            scores = lax.dot_general(
-                only, kv[:, :inner], (((1,), (1,)), ((), ())), preferred_element_type=jnp.float32
-            )
-            weights = jnp.exp(scores + bias)
-            denominator = jnp.sum(weights, axis=1, keepdims=True)
-            numerator = jnp.dot(
-                weights.astype(jnp.bfloat16), kv[:, inner : 2 * inner], preferred_element_type=jnp.float32
-            )
-            attended = jnp.where(head_of == head, numerator / denominator, attended)
+        ratio = numerator / denominator
+        attended = ratio[:tokens]
+        for j in range(1, own_heads):
+            attended = jnp.where(head_of == j, ratio[j * tokens : (j + 1) * tokens], attended)
         att[c] = attended.astype(jnp.bfloat16)
 
     def term(c, slot):
@@ -271,6 +281,8 @@
                 qj = wrap(q + k, seqs)
                 theirs = kv.at[pl.ds(pl.multiple_of(qj * shard, shard), shard)]
                 arrived(theirs, kv_send.at[0], kv_recv.at[qj])
+        if c == 0:
+            prepare()
         attend(c, query)
         if c == 0:
             loads["wo"].wait()
@@ -294,7 +306,9 @@
     all_tokens, width = hidden.shape[1:]
     tokens = all_tokens // CHUNKS
     rows_each, model = memory.shape
-    padded = (rows_each + 1 + 15) // 16 * 16
+    padded = 16
+    while padded < rows_each + 1:
+        padded *= 2
     inner = w_query.shape[2]
     flags = jnp.pad(keep.astype(jnp.bfloat16)[None, :], ((0, 0), (0, model - rows_each)))
     block = jnp.concatenate(
@@ -302,7 +316,7 @@
     )
     shard = sections * heads * rows_each
     low = jnp.bfloat16
-    hbm = pl.BlockSpec(memory_space=pl.ANY)
+    hbm = pl.BlockSpec(memory_space=pltpu.HBM)
     dma = pltpu.SemaphoreType.DMA
     return pl.pallas_call(
         functools.partial(kernel, sections, seqs, heads, rows_each),
@@ -320,6 +334,8 @@
             pltpu.VMEM((sections * heads * padded, 2 * inner + 128), low),
             pltpu.VMEM((seqs * shard, 2 * inner + 128), low),
             pltpu.VMEM((CHUNKS, tokens, inner), low),
+            pltpu.VMEM((inner, seqs * shard), low),
+            pltpu.VMEM((8, seqs * shard), jnp.float32),
             pltpu.VMEM((CHUNKS, lines, tokens, width), low),
             pltpu.VMEM((CHUNKS, lines, tokens, width), low),
             pltpu.VMEM((CHUNKS, lines, tokens, width), low),

time: 84.2 us -> 82.1 us (0.975)
  Pallas kernels: 76 us -> 74.5 us
    pallas_call x1, Pallas kernels: 76 us -> 74.5 us  [shards(): pl.pallas_call(functools.partial(kernel, sections, seqs, heads, rows_each...]
where the time goes in v2:
time: 82.1 us; the launch traced here: 81.8 us
  Pallas kernels  74.5 us (91%)
  local copies, waits for them, and re-layouts  5.63 us (7%)
  other arithmetic  1.65 us (2%)
    pallas_call x1, Pallas kernels, shards(): pl.pallas_call(functools.partial(kernel, sections, seqs, heads, rows_each...  74.5 us
    unnamed x9, local copies, waits for them, and re-layouts  5.55 us

profile of v2, /device:TPU:1, one launch (start us, length us, event | category | flops | bytes accessed | tf_op | source)
XLA Modules:
  0.0 81.8 jit_solution(10827665011058905048)
XLA Ops:
  0.0 0.7 convert_bitcast_fusion
  0.7 0.1 pad.7.clone
  0.7 1.0 %fusion.3.mem_ref = bf16[16,4096]{1,0:T(8,128)(2,1)S(1)} fusion(bf16[1,12]{1,0:T(2,128)(2,1)S(1)} %convert_bitcast_fusion, bf16[12,4096]{1,0:T(8,128)(2,1)} %param.14, bf16[16]{0:T(256)(128)(2,1)S(1)} %pad.7.clone), kind=kLoop, calls=%fused_computation.5 | loop fusion | flops 655360 | bytes 229432 | tf_op jit(solution)/shard_map/concatenate | solution.py:314
  1.7 0.0 copy-start
  1.7 1.6 %copy-done = bf16[1,4096,256]{2,1,0:T(8,128)(2,1)S(1)} copy-done((bf16[1,4096,256]{2,1,0:T(8,128)(2,1)S(1)}, bf16[1,4096,256]{2,1,0:T(8,128)(2,1)}, u32[]{:S(2)}) %copy-start) | copy-done | bytes 2097176
  3.3 0.0 copy-start.1
  3.3 1.6 %copy-done.1 = bf16[1,4096,256]{2,1,0:T(8,128)(2,1)S(1)} copy-done((bf16[1,4096,256]{2,1,0:T(8,128)(2,1)S(1)}, bf16[1,4096,256]{2,1,0:T(8,128)(2,1)}, u32[]{:S(2)}) %copy-start.1) | copy-done | bytes 2097176
  4.9 0.0 copy-start.2
  4.9 0.9 %copy-done.2 = bf16[1,256,512]{2,1,0:T(8,128)(2,1)S(1)} copy-done((bf16[1,256,512]{2,1,0:T(8,128)(2,1)S(1)}, bf16[1,256,512]{2,1,0:T(8,128)(2,1)}, u32[]{:S(2)}) %copy-start.2) | copy-done | bytes 262168
  5.9 0.0 copy-start.3
  5.9 0.7 copy-done.3
  6.6 74.5 %shard_map.82 = bf16[256,512]{1,0:T(8,128)(2,1)S(1)} custom-call(bf16[256,512]{1,0:T(8,128)(2,1)S(1)} %bitcast.11, bf16[1,4096]{1,0:T(2,128)(2,1)S(1)} %copy-done.3, bf16[4096,256]{1,0:T(8,128)(2,1)S(1)} %bitcast.8, bf16[4096,256]{1,0:T(8,128)(2,1)S(1)} %bitcast.9, bf16[4096,256]{1,0:T(8,128)(2,1)} %bitcast.12, bf16[256,4096]{1,0:T(8,128)(2,1)} %bitcast.13, ...), custom_call_target="tpu_custom_call" | custom-call | tf_op jit(solution)/shard_map/pallas_call | solution.py:321
  81.1 0.7 copy.10
  (1 shorter events, 0.0 us)
Async XLA Ops:
  1.7 1.6 %copy-start = (bf16[1,4096,256]{2,1,0:T(8,128)(2,1)S(1)}, bf16[1,4096,256]{2,1,0:T(8,128)(2,1)}, u32[]{:S(2)}) copy-start(bf16[1,4096,256]{2,1,0:T(8,128)(2,1)} %param.10) | copy-start | bytes 6291460
  3.3 1.6 %copy-start.1 = (bf16[1,4096,256]{2,1,0:T(8,128)(2,1)S(1)}, bf16[1,4096,256]{2,1,0:T(8,128)(2,1)}, u32[]{:S(2)}) copy-start(bf16[1,4096,256]{2,1,0:T(8,128)(2,1)} %param.11) | copy-start | bytes 6291460
  4.9 0.9 %copy-start.2 = (bf16[1,256,512]{2,1,0:T(8,128)(2,1)S(1)}, bf16[1,256,512]{2,1,0:T(8,128)(2,1)}, u32[]{:S(2)}) copy-start(bf16[1,256,512]{2,1,0:T(8,128)(2,1)} %param.8) | copy-start | bytes 786436
  5.9 0.7 copy-start.3

commit v3 on v2

--- a/solution.py
+++ b/solution.py
@@ -162,6 +162,9 @@
         arrived(mem.at[s, slot], mem_send.at[0], mem_recv.at[s, slot])
         mem_across(mem.at[s, slot], slot, lines + k)
 
+    for c in range(1, min(CHUNKS, 2)):
+        hid_forward(c)
+
     loads["mem"].wait()
     loads["wk"].wait()
     loads["wv"].wait()
@@ -273,8 +276,8 @@
         if c == 0:
             loads["wq"].wait()
             loads["gain"].wait()
-        if c + 1 < CHUNKS:
-            hid_forward(c + 1)
+        if c + 2 < CHUNKS:
+            hid_forward(c + 2)
         query = query_of(c)
         if c == 0:
             for k in range(1, seqs):

time: 82.1 us -> 83.5 us (1.017)
  Pallas kernels: 74.5 us -> 75.9 us
    pallas_call x1, Pallas kernels: 74.5 us -> 75.9 us  [shards(): pl.pallas_call(functools.partial(kernel, sections, seqs, heads, rows_each...]
where the time goes in v3:
time: 83.5 us; the launch traced here: 83.2 us
  Pallas kernels  75.9 us (91%)
  local copies, waits for them, and re-layouts  5.63 us (7%)
  other arithmetic  1.65 us (2%)
    pallas_call x1, Pallas kernels, shards(): pl.pallas_call(functools.partial(kernel, sections, seqs, heads, rows_each...  75.9 us
    unnamed x9, local copies, waits for them, and re-layouts  5.55 us

profile of v3, /device:TPU:1, one launch (start us, length us, event | category | flops | bytes accessed | tf_op | source)
XLA Modules:
  0.0 83.2 jit_solution(2577435863800742138)
XLA Ops:
  0.0 0.7 convert_bitcast_fusion
  0.7 0.1 pad.7.clone
  0.7 1.0 %fusion.3.mem_ref = bf16[16,4096]{1,0:T(8,128)(2,1)S(1)} fusion(bf16[1,12]{1,0:T(2,128)(2,1)S(1)} %convert_bitcast_fusion, bf16[12,4096]{1,0:T(8,128)(2,1)} %param.14, bf16[16]{0:T(256)(128)(2,1)S(1)} %pad.7.clone), kind=kLoop, calls=%fused_computation.5 | loop fusion | flops 655360 | bytes 229432 | tf_op jit(solution)/shard_map/concatenate | solution.py:317
  1.7 0.0 copy-start
  1.7 1.6 %copy-done = bf16[1,4096,256]{2,1,0:T(8,128)(2,1)S(1)} copy-done((bf16[1,4096,256]{2,1,0:T(8,128)(2,1)S(1)}, bf16[1,4096,256]{2,1,0:T(8,128)(2,1)}, u32[]{:S(2)}) %copy-start) | copy-done | bytes 2097176
  3.3 0.0 copy-start.1
  3.3 1.6 %copy-done.1 = bf16[1,4096,256]{2,1,0:T(8,128)(2,1)S(1)} copy-done((bf16[1,4096,256]{2,1,0:T(8,128)(2,1)S(1)}, bf16[1,4096,256]{2,1,0:T(8,128)(2,1)}, u32[]{:S(2)}) %copy-start.1) | copy-done | bytes 2097176
  4.9 0.0 copy-start.2
  4.9 0.9 %copy-done.2 = bf16[1,256,512]{2,1,0:T(8,128)(2,1)S(1)} copy-done((bf16[1,256,512]{2,1,0:T(8,128)(2,1)S(1)}, bf16[1,256,512]{2,1,0:T(8,128)(2,1)}, u32[]{:S(2)}) %copy-start.2) | copy-done | bytes 262168
  5.9 0.0 copy-start.3
  5.9 0.7 copy-done.3
  6.6 75.9 %shard_map.82 = bf16[256,512]{1,0:T(8,128)(2,1)S(1)} custom-call(bf16[256,512]{1,0:T(8,128)(2,1)S(1)} %bitcast.11, bf16[1,4096]{1,0:T(2,128)(2,1)S(1)} %copy-done.3, bf16[4096,256]{1,0:T(8,128)(2,1)S(1)} %bitcast.8, bf16[4096,256]{1,0:T(8,128)(2,1)S(1)} %bitcast.9, bf16[4096,256]{1,0:T(8,128)(2,1)} %bitcast.12, bf16[256,4096]{1,0:T(8,128)(2,1)} %bitcast.13, ...), custom_call_target="tpu_custom_call" | custom-call | tf_op jit(solution)/shard_map/pallas_call | solution.py:324
  82.5 0.7 copy.10
  (1 shorter events, 0.0 us)
Async XLA Ops:
  1.7 1.6 %copy-start = (bf16[1,4096,256]{2,1,0:T(8,128)(2,1)S(1)}, bf16[1,4096,256]{2,1,0:T(8,128)(2,1)}, u32[]{:S(2)}) copy-start(bf16[1,4096,256]{2,1,0:T(8,128)(2,1)} %param.10) | copy-start | bytes 6291460
  3.3 1.6 %copy-start.1 = (bf16[1,4096,256]{2,1,0:T(8,128)(2,1)S(1)}, bf16[1,4096,256]{2,1,0:T(8,128)(2,1)}, u32[]{:S(2)}) copy-start(bf16[1,4096,256]{2,1,0:T(8,128)(2,1)} %param.11) | copy-start | bytes 6291460
  4.9 0.9 %copy-start.2 = (bf16[1,256,512]{2,1,0:T(8,128)(2,1)S(1)}, bf16[1,256,512]{2,1,0:T(8,128)(2,1)}, u32[]{:S(2)}) copy-start(bf16[1,256,512]{2,1,0:T(8,128)(2,1)} %param.8) | copy-start | bytes 786436
  5.9 0.7 copy-start.3
